TPU v7x, 512 devices: a whole 4x8x8 slice. The times are simulated.
512 devices in a mesh: grp: 32 (over y_hi, z, core), lane: 16 (over x, y_lo).
Axes of the slice: x: 4, y: 8 (y_hi: 2, y_lo: 4; y = y_hi * 4 + y_lo), z: 8, core: 2. Of those that a mesh axis runs over, the one named last changes fastest.
Arguments:
- passage_query: bfloat16 [32, 16, 3, 128, 2048], P('grp', 'lane'), may hold values from -6 to 6
- passage_keyval: bfloat16 [32, 16, 3, 2, 128, 1024], P('grp', 'lane'), may hold values from -12 to 12
- prefix_keys: bfloat16 [32, 1024, 1024], P('grp', 'lane'), may hold values from -16 to 16
- prefix_values: bfloat16 [32, 1024, 1024], P('grp', 'lane'), may hold values from -6 to 6
- home_count: int32 [32, 16], P('grp', 'lane'), may hold values from 1 to 3, as said below
- move_slot: int32 [32, 16], P('grp', 'lane'), may hold values from 0 to 3, as said below
- score_weight: bfloat16 [2048], replicated, may hold values from -0.125 to 0.125
Outputs:
- attended: bfloat16 [32, 16, 2, 128, 2048], P('grp', 'lane')
- scores: float32 [32, 16, 3], P('grp', 'lane')
Inputs may be any that keep to these rules, and one draw needn't show every extreme that they name: Home slots 0 .. home_count - 1 of device (g, l) hold passages of query g; some device holds 3. `move_slot`: a live home slot of (g, l) whose passage runs on device (g+1 mod 32, l), or 3 for none; on every device the kept passages plus the one received are at most 2, and some device runs 2.
All inputs are finite; a program needn't handle non-finite values.
Results may differ from a plain program's by a relative error of at most 0.009.
Values may be sent and summed in bfloat16 or wider, within the bound.
A program may use at most 128 MiB of HBM per device.

v0:
```python
import jax
import jax.numpy as jnp
from jax import lax
from jax.sharding import PartitionSpec as P

HD = 256


softcap = 50.0


def from_behind(x, axis, by):
    devices = lax.axis_size(axis)
    return lax.ppermute(x, axis, [(i, (i + by) % devices) for i in range(devices)])


def block_terms(query_rows, key_rows, value_rows, allowed):
    slot_count, tokens, row_width = query_rows.shape
    kv_heads = key_rows.shape[2] // HD
    group_size = row_width // HD // kv_heads
    queries = query_rows.reshape(slot_count, tokens, kv_heads, group_size, HD)
    key_split = key_rows.reshape(slot_count, key_rows.shape[1], kv_heads, HD)
    value_split = value_rows.reshape(slot_count, value_rows.shape[1], kv_heads, HD)
    products = jnp.einsum(
        "stgrd,sugd->sgrtu", queries, key_split, preferred_element_type=jnp.float32
    ) * HD ** (-0.5)
    exponent = jnp.exp(softcap * jnp.tanh(products / softcap))
    if allowed is not None:
        exponent = jnp.where(allowed, exponent, 0.0)
    numerator = jnp.einsum(
        "sgrtu,sugd->stgrd",
        exponent.astype(jnp.bfloat16),
        value_split,
        preferred_element_type=jnp.float32,
    )
    return (numerator.reshape(slot_count, tokens, row_width), jnp.sum(exponent, axis=-1))


def body(
    passage_query, passage_keyval, prefix_keys, prefix_values, home_count, move_slot, score_weight
):
    query_home = passage_query[0, 0]
    keyval_home = passage_keyval[0, 0]
    live_count = home_count[0, 0]
    move_index = move_slot[0, 0]
    home_slots = query_home.shape[0]
    run_slots = home_slots - 1
    tokens = query_home.shape[1]
    moved_flag = move_index < home_slots
    pick_slot = jnp.minimum(move_index, home_slots - 1)
    sent_flag = moved_flag.astype(jnp.bfloat16).reshape(1)
    sent_query = lax.dynamic_index_in_dim(query_home, pick_slot, 0, keepdims=False)
    sent_keyval = lax.dynamic_index_in_dim(keyval_home, pick_slot, 0, keepdims=False)
    own_keys = prefix_keys[0]
    own_values = prefix_values[0]
    guest_query, guest_keyval, guest_flag, guest_keys, guest_values = from_behind(
        (sent_query, sent_keyval, sent_flag, own_keys, own_values), "grp", 1
    )
    kept_count = live_count - moved_flag.astype(jnp.int32)
    run_index = jnp.arange(run_slots, dtype=jnp.int32)
    own_source = run_index + (run_index >= move_index).astype(jnp.int32)
    is_own = run_index < kept_count
    is_guest = (run_index == kept_count) & (guest_flag[0] > 0)
    run_query = jnp.where(
        is_guest[:, None, None], guest_query[None], jnp.take(query_home, own_source, axis=0)
    )
    run_keyval = jnp.where(
        is_guest[:, None, None, None], guest_keyval[None], jnp.take(keyval_home, own_source, axis=0)
    )
    positions = jnp.arange(tokens, dtype=jnp.int32)
    allowed = positions[None, :] <= positions[:, None]
    numerator, denominator = block_terms(run_query, run_keyval[:, 0], run_keyval[:, 1], allowed)
    own_kpiece = lax.all_gather(own_keys, "lane", axis=0, tiled=True)
    own_vpiece = lax.all_gather(own_values, "lane", axis=0, tiled=True)
    guest_kpiece = lax.all_gather(guest_keys, "lane", axis=0, tiled=True)
    guest_vpiece = lax.all_gather(guest_values, "lane", axis=0, tiled=True)
    key_rows = jnp.where(is_guest[:, None, None], guest_kpiece[None], own_kpiece[None])
    value_rows = jnp.where(is_guest[:, None, None], guest_vpiece[None], own_vpiece[None])
    part_numerator, part_denominator = block_terms(run_query, key_rows, value_rows, None)
    numerator, denominator = (numerator + part_numerator, denominator + part_denominator)
    head_totals = jnp.transpose(denominator, (0, 3, 1, 2)).reshape(run_slots, tokens, -1)
    head_count = head_totals.shape[2]
    result = numerator.reshape(run_slots, tokens, head_count, HD) / head_totals[..., None]
    live_slot = (is_own | is_guest)[:, None, None]
    attended = jnp.where(live_slot, result.reshape(run_slots, tokens, -1), 0.0).astype(jnp.bfloat16)
    slot_score = jnp.dot(
        attended[:, tokens - 1, :], score_weight, preferred_element_type=jnp.float32
    )
    guest_score = slot_score[jnp.minimum(kept_count, run_slots - 1)].reshape(1)
    returned = from_behind(guest_score, "grp", -1)
    home_index = jnp.arange(home_slots, dtype=jnp.int32)
    run_place = jnp.clip(home_index - (home_index > move_index).astype(jnp.int32), 0, run_slots - 1)
    own_score = jnp.take(slot_score, run_place)
    scores = jnp.where(
        home_index == move_index, returned[0], jnp.where(home_index < live_count, own_score, 0.0)
    )
    return (attended[None, None], scores[None, None])


def solution(mesh):
    in_specs = (
        P("grp", "lane", None, None, None),
        P("grp", "lane", None, None, None, None),
        P("grp", "lane", None),
        P("grp", "lane", None),
        P("grp", "lane"),
        P("grp", "lane"),
        P(),
    )
    out_specs = (P("grp", "lane", None, None, None), P("grp", "lane", None))
    return jax.shard_map(body, mesh=mesh, in_specs=in_specs, out_specs=out_specs, check_vma=False)
```

profile of v0, /device:TPU:1, one launch (start us, length us, event | category | flops | bytes accessed | tf_op | source)
XLA Modules:
  0.0 418.9 jit_solution(4349812735515382883)
XLA Ops:
  8.7 5.4 %collective-permute-start.4 = (bf16[64,1024]{1,0:T(8,128)(2,1)}, bf16[64,1024]{1,0:T(8,128)(2,1)S(1)}, u32[]{:S(2)}, u32[]{:S(2)}) collective-permute-start(bf16[64,1024]{1,0:T(8,128)(2,1)} %bitcast.96), channel_id=1, source_target_pairs={{0,16},{16,32},{32,48},{48,64},{64,80},{80,96},{96,112},{112,128},... | collective-permute-start | bytes 393224 | tf_op jit(solution)/shard_map/ppermute | solution.py:14
  14.1 4.4 %collective-permute-done.4 = bf16[64,1024]{1,0:T(8,128)(2,1)S(1)} collective-permute-done((bf16[64,1024]{1,0:T(8,128)(2,1)}, bf16[64,1024]{1,0:T(8,128)(2,1)S(1)}, u32[]{:S(2)}, u32[]{:S(2)}) %collective-permute-start.4) | collective-permute-done | bytes 131104 | tf_op jit(solution)/shard_map/ppermute | solution.py:14
  19.3 2.1 collective-permute-start.3
  21.3 12.5 %collective-permute-done.3 = bf16[64,1024]{1,0:T(8,128)(2,1)S(1)} collective-permute-done((bf16[64,1024]{1,0:T(8,128)(2,1)}, bf16[64,1024]{1,0:T(8,128)(2,1)S(1)}, u32[]{:S(2)}, u32[]{:S(2)}) %collective-permute-start.3) | collective-permute-done | bytes 131104 | tf_op jit(solution)/shard_map/ppermute | solution.py:14
  36.0 1.9 collective-permute-start.1
  37.9 6.4 %collective-permute-start = (bf16[1]{0:T(256)(128)(2,1)}, bf16[1]{0:T(256)(128)(2,1)}, u32[]{:S(2)}, u32[]{:S(2)}) collective-permute-start(bf16[1]{0:T(256)(128)(2,1)} %bitcast.2), channel_id=1, source_target_pairs={{0,16},{16,32},{32,48},{48,64},{64,80},{80,96},{96,112},{112,128},... | collective-permute-start | bytes 14 | tf_op jit(solution)/shard_map/ppermute | solution.py:14
  46.4 1.9 collective-permute-start.2
  49.7 3.0 gather_fusion.1
  52.7 2.6 gather.18
  57.3 1.2 copy.38
  58.8 2.3 fusion.40
  61.1 1.8 fusion.23
  62.9 33.8 %all-gather.13.cloned.1.call-done = bf16[1,1024,1024]{2,1,0:T(8,128)(2,1)} async-done(((bf16[1,64,1024]{2,1,0:T(8,128)(2,1)}), bf16[1,1024,1024]{2,1,0:T(8,128)(2,1)}) %all-gather.13.cloned.1.call-update) | async-done | bytes 2097168 | tf_op jit(solution)/shard_map/all_gather | solution.py:73
  96.7 3.9 copy.63
  100.6 90.4 %all-gather.11.cloned.1.call-done = bf16[1,1024,1024]{2,1,0:T(8,128)(2,1)} async-done(((bf16[1,64,1024]{2,1,0:T(8,128)(2,1)}), bf16[1,1024,1024]{2,1,0:T(8,128)(2,1)}) %all-gather.11.cloned.1.call-update) | async-done | bytes 2097168 | tf_op jit(solution)/shard_map/all_gather | solution.py:74
  190.9 4.0 copy.61
  194.9 87.3 %all-gather.9.cloned.1.call-done = bf16[1024,1024]{1,0:T(8,128)(2,1)} async-done(((bf16[64,1024]{1,0:T(8,128)(2,1)}), bf16[1024,1024]{1,0:T(8,128)(2,1)}) %all-gather.9.cloned.1.call-update) | async-done | bytes 2097168 | tf_op jit(solution)/shard_map/all_gather | solution.py:75
  282.2 3.9 copy.62
  286.2 7.3 %bitcast_reduce_fusion = (f32[2,4,2,128]{3,2,1,0:T(2,128)S(1)}, f32[2,4,1024,128,2]{3,2,4,1,0:T(8,128)}) fusion(bf16[2,128,4,2,256]{4,3,2,1,0:T(2,128)(2,1)S(1)} %copy-done.2, pred[2]{0:T(512)(128)(4,1)S(1)} %compare_and_fusion, pred[2]{0:T(512)(128)(4,1)S(1)} %compare_and_fusion.1, bf16[128,4,2,256]{3,0,2,1:T(8,128)(2,1)S(1)} %copy.38, ...), kind=kOutput, calls=%fused_computation.3 | convolution fusion | flops 1083176960 | bytes 14163972 | tf_op jit(solution)/shard_map/stgrd,sugd->sgrtu/dot_general | solution.py:24
  293.6 1.6 div.39
  295.3 2.7 reshape.260
  298.0 2.7 div.40
  300.7 72.7 %all-gather.7.cloned.1.call-done = bf16[1024,1024]{1,0:T(8,128)(2,1)} async-done(((bf16[64,1024]{1,0:T(8,128)(2,1)}), bf16[1024,1024]{1,0:T(8,128)(2,1)}) %all-gather.7.cloned.1.call-update) | async-done | bytes 2097168 | tf_op jit(solution)/shard_map/all_gather | solution.py:76
  373.4 3.9 copy.60
  377.3 8.2 %fusion.14 = f32[2,4,256,2,128]{4,2,3,1,0:T(8,128)S(1)} fusion(f32[2,4,256,2,128]{4,2,3,1,0:T(8,128)} %fusion.23, f32[2,4,1024,128,2]{3,2,4,1,0:T(8,128)} %get-tuple-element.7, pred[2]{0:T(512)(128)(4,1)S(1)} %compare_and_fusion.1, bf16[1024,4,256]{0,2,1:T(8,128)(2,1)} %bitcast.89, bf16[1024,4,256]{0,2,1:T(8,128)(2,1)} %bitcast.92), kind=kOutput, calls=%fused_computation.21 | convolution fusion | flops 1082654720 | bytes 16777218 | tf_op jit(solution)/shard_map/sgrtu,sugd->stgrd/dot_general | solution.py:30
  385.5 1.3 copy-done.1
  386.8 1.9 slice.20
  388.7 2.2 copy.67
  392.6 11.4 %collective-permute-start.5 = (f32[1]{0:T(128)}, f32[1]{0:T(128)}, u32[]{:S(2)}, u32[]{:S(2)}) collective-permute-start(f32[1]{0:T(128)} %dynamic_slice.13), channel_id=1, source_target_pairs={{0,496},{16,0},{32,16},{48,32},{64,48},{80,64},{96,80},{112,96},{1... | collective-permute-start | bytes 20 | tf_op jit(solution)/shard_map/ppermute | solution.py:14
  404.7 2.9 copy.49
  407.6 3.6 select_convert_fusion
  411.2 1.1 compare_select_fusion.5
  (46 shorter events, 10.6 us)
Async XLA Ops:
  7.2 27.9 %copy-start = (bf16[1,1,3,2,128,1024]{5,4,3,2,1,0:T(8,128)(2,1)S(1)}, bf16[1,1,3,2,128,1024]{5,4,3,2,1,0:T(8,128)(2,1)}, u32[]{:S(2)}) copy-start(bf16[1,1,3,2,128,1024]{5,4,3,2,1,0:T(8,128)(2,1)} %param.8) | copy-start | bytes 4718596
  7.2 89.5 %all-gather.13.cloned.1.call-start = ((), (), s32[]{:S(2)}) async-start(), calls=%async_computation.3 | async-start | bytes 2228224 | tf_op jit(solution)/shard_map/all_gather | solution.py:73
  7.9 183.0 %all-gather.11.cloned.1.call-start = ((), (), s32[]{:S(2)}) async-start(), calls=%async_computation.2 | async-start | bytes 2228224 | tf_op jit(solution)/shard_map/all_gather | solution.py:74
  8.7 273.6 %all-gather.9.cloned.1.call-start = ((), (), s32[]{:S(2)}) async-start(), calls=%async_computation.1 | async-start | bytes 2228224 | tf_op jit(solution)/shard_map/all_gather | solution.py:75
  8.7 9.8 %collective-permute-start.4 = (bf16[64,1024]{1,0:T(8,128)(2,1)}, bf16[64,1024]{1,0:T(8,128)(2,1)S(1)}, u32[]{:S(2)}, u32[]{:S(2)}) collective-permute-start(bf16[64,1024]{1,0:T(8,128)(2,1)} %bitcast.96), channel_id=1, source_target_pairs={{0,16},{16,32},{32,48},{48,64},{64,80},{80,96},{96,112},{112,128},... | collective-permute-start | bytes 393224 | tf_op jit(solution)/shard_map/ppermute | solution.py:14
  18.5 0.6 copy-start.4
  19.2 354.2 %all-gather.7.cloned.1.call-start = ((), (), s32[]{:S(2)}) async-start(), calls=%async_computation | async-start | bytes 2228224 | tf_op jit(solution)/shard_map/all_gather | solution.py:76
  19.3 14.5 %collective-permute-start.3 = (bf16[64,1024]{1,0:T(8,128)(2,1)}, bf16[64,1024]{1,0:T(8,128)(2,1)S(1)}, u32[]{:S(2)}, u32[]{:S(2)}) collective-permute-start(bf16[64,1024]{1,0:T(8,128)(2,1)} %bitcast.97), channel_id=1, source_target_pairs={{0,16},{16,32},{32,48},{48,64},{64,80},{80,96},{96,112},{112,128},... | collective-permute-start | bytes 393224 | tf_op jit(solution)/shard_map/ppermute | solution.py:14
  33.8 0.6 copy-start.3
  36.0 20.1 %collective-permute-start.1 = (bf16[2,128,1024]{2,1,0:T(8,128)(2,1)}, bf16[2,128,1024]{2,1,0:T(8,128)(2,1)S(1)}, u32[]{:S(2)}, u32[]{:S(2)}) collective-permute-start(bf16[2,128,1024]{2,1,0:T(8,128)(2,1)} %dynamic-slice_bitcast_fusion), channel_id=1, source_target_pairs={{0,16},{16,32},{32,48},{48,64},{64,80},{80,96},{96,112},{112,128},... | collective-permute-start | bytes 1572872 | tf_op jit(solution)/shard_map/ppermute | solution.py:14
  37.9 17.5 %collective-permute-start = (bf16[1]{0:T(256)(128)(2,1)}, bf16[1]{0:T(256)(128)(2,1)}, u32[]{:S(2)}, u32[]{:S(2)}) collective-permute-start(bf16[1]{0:T(256)(128)(2,1)} %bitcast.2), channel_id=1, source_target_pairs={{0,16},{16,32},{32,48},{48,64},{64,80},{80,96},{96,112},{112,128},... | collective-permute-start | bytes 14 | tf_op jit(solution)/shard_map/ppermute | solution.py:14
  46.4 10.9 %collective-permute-start.2 = (bf16[128,2048]{0,1:T(8,128)(2,1)}, bf16[128,2048]{0,1:T(8,128)(2,1)}, u32[]{:S(2)}, u32[]{:S(2)}) collective-permute-start(bf16[128,2048]{0,1:T(8,128)(2,1)} %bitcast.12), channel_id=1, source_target_pairs={{0,16},{16,32},{32,48},{48,64},{64,80},{80,96},{96,112},{112,128},... | collective-permute-start | bytes 1572872 | tf_op jit(solution)/shard_map/ppermute | solution.py:14
  49.6 5.6 %copy-start.5 = (bf16[2048]{0:T(1024)(128)(2,1)S(1)}, bf16[2048]{0:T(1024)(128)(2,1)}, u32[]{:S(2)}) copy-start(bf16[2048]{0:T(1024)(128)(2,1)} %param.13) | copy-start | bytes 12292
  194.9 91.3 %copy-start.2 = (bf16[2,128,4,2,256]{4,3,2,1,0:T(2,128)(2,1)S(1)}, bf16[2,128,4,2,256]{4,3,2,1,0:T(2,128)(2,1)}, u32[]{:S(2)}) copy-start(bf16[2,128,4,2,256]{4,3,2,1,0:T(2,128)(2,1)} %gather.18) | copy-start | bytes 3145732
  385.4 1.3 copy-start.1
  392.6 18.6 %collective-permute-start.5 = (f32[1]{0:T(128)}, f32[1]{0:T(128)}, u32[]{:S(2)}, u32[]{:S(2)}) collective-permute-start(f32[1]{0:T(128)} %dynamic_slice.13), channel_id=1, source_target_pairs={{0,496},{16,0},{32,16},{48,32},{64,48},{80,64},{96,80},{112,96},{1... | collective-permute-start | bytes 20 | tf_op jit(solution)/shard_map/ppermute | solution.py:14
Sparse Core Ops, SparseCore 0:
  10.1 86.5 all-gather.12
  98.7 92.1 all-gather.10
  193.0 89.1 all-gather.8
  284.2 89.1 all-gather.6
where the time goes:
time: 420 us; the launch traced here: 419 us
  waiting for transfers between devices  302 us (72%)
  local copies, waits for them, and re-layouts  46.6 us (11%)
  starting transfers between devices  29.3 us (7%)
  matrix products  19.7 us (5%)
  between operations  15.9 us (4%)
  other arithmetic  5.03 us (1%)
    all_gather x1, waiting for transfers between devices, body(): own_vpiece = lax.all_gather(own_values, 'lane', axis=0, tiled=True)  90.4 us
    all_gather x1, waiting for transfers between devices, body(): guest_kpiece = lax.all_gather(guest_keys, 'lane', axis=0, tiled=True)  87.3 us
    all_gather x1, waiting for transfers between devices, body(): guest_vpiece = lax.all_gather(guest_values, 'lane', axis=0, tiled=True)  72.7 us
    all_gather x1, waiting for transfers between devices, body(): own_kpiece = lax.all_gather(own_keys, 'lane', axis=0, tiled=True)  33.8 us
    ppermute x6, starting transfers between devices, from_behind(): lax.ppermute(x, axis, [(i, (i + by) % devices) for i in range(devices)])  29.1 us
    ppermute x6, waiting for transfers between devices, from_behind(): lax.ppermute(x, axis, [(i, (i + by) % devices) for i in range(devices)])  16.9 us
    dot_general x2, matrix products, block_terms(): jnp.einsum('sgrtu,sugd->stgrd', exponent.astype(jnp.bfloat16), value_spli...  9.9 us
    dot_general x2, matrix products, block_terms(): jnp.einsum('stgrd,sugd->sgrtu', queries, key_split, preferred_element_typ...  9.59 us
  transfers between devices with their start and end apart: 10, of which 6 were waited for; matrix products, arithmetic and copies ran while one was open for 12% of the time, Pallas kernels for 0%

commit v1 on v0

v1 whole, which is shorter than its diff:
```python
import functools

import jax
import jax.numpy as jnp
from jax import lax
from jax.experimental import pallas as pl
from jax.experimental.pallas import tpu as pltpu
from jax.sharding import PartitionSpec as P

MESH = pl.DeviceIdType.MESH
HD = 256
KVH = 4
SIDE = 4
SOFTCAP = 50.0
NT = (((1,), (1,)), ((), ()))


def kernel(
    query_ref, keyval_ref, pkeys_ref, pvalues_ref, count_ref, move_ref, weight_ref,
    att_ref, score_ref,
    kbuf, vbuf, query, keyval, num, den, own, sent, guest, sums,
    load_sem, y_send, x_send, relay_send, y_recv, x_recv, relay_recv, g_send, g_recv,
):
    groups = lax.axis_size("grp")
    g = lax.axis_index("grp")
    lane = lax.axis_index("lane")
    x, y = lane // SIDE, lax.rem(lane, SIDE)
    tokens = query.shape[1]
    rows = pkeys_ref.shape[0]
    col = rows * SIDE
    bufs = (kbuf, vbuf)

    right = (g, lax.rem(x + 1, SIDE) * SIDE + y)
    left = (g, lax.rem(x + 3, SIDE) * SIDE + y)
    above = [(g, x * SIDE + lax.rem(y + d, SIDE)) for d in (1, 2, 3)]
    ahead = (lax.rem(g + 1, groups), lane)
    behind = (lax.rem(g + groups - 1, groups), lane)

    barrier = pltpu.get_barrier_semaphore()
    for other in (right, left, *above, ahead, behind):
        pl.semaphore_signal(barrier, inc=1, device_id=other, device_id_type=MESH)

    def block(xx, yy):
        return pl.ds(pl.multiple_of((xx * SIDE + yy) * rows, rows), rows)

    loads = []
    for h in range(KVH):
        for kv, ref in enumerate((pkeys_ref, pvalues_ref)):
            loads.append(pltpu.make_async_copy(
                ref.at[:, pl.ds(h * HD, HD)], bufs[kv].at[h, block(x, y)], load_sem.at[h * 2 + kv]))
    loads.append(pltpu.make_async_copy(query_ref, query, load_sem.at[8]))
    loads.append(pltpu.make_async_copy(keyval_ref, keyval, load_sem.at[9]))
    for c in loads:
        c.start()

    move = move_ref[0, 0]
    count = count_ref[0, 0]
    moved = (move < 3).astype(jnp.int32)
    kept = count - moved
    source = [jnp.minimum(move, 2)] + [j + (j >= move).astype(jnp.int32) for j in (0, 1)]

    def remote(h, kv, xx, yy, send_sem, recv_sem, to):
        ref = bufs[kv].at[h, block(xx, yy)]
        return pltpu.make_async_remote_copy(
            src_ref=ref, dst_ref=ref, send_sem=send_sem, recv_sem=recv_sem,
            device_id=to, device_id_type=MESH)

    def y_copy(h, kv, d):
        return remote(h, kv, x, y, y_send.at[h, kv, d - 1], y_recv.at[h, kv, y], above[d - 1])

    def x_copy(h, kv, yy, side):
        return remote(h, kv, x, yy, x_send.at[h, kv, yy, side], x_recv.at[h, kv, yy, side],
                      (right, left)[side])

    def relay_copy(h, kv, yy):
        xx = lax.rem(x + (3, 1)[kv], SIDE)
        return remote(h, kv, xx, yy, relay_send.at[h, kv, yy], relay_recv.at[h, kv, yy], (right, left)[kv])

    def wait_y(h, kv, d):
        yy = lax.rem(y + d, SIDE)
        remote(h, kv, x, yy, y_send.at[h, kv, 0], y_recv.at[h, kv, yy], right).wait_recv()
        return yy

    def wait_x(h, kv, yy, side):
        xx = lax.rem(x + (3, 1)[side], SIDE)
        remote(h, kv, xx, yy, x_send.at[h, kv, yy, side], x_recv.at[h, kv, yy, side], right).wait_recv()

    def wait_relay(h, kv, yy):
        xx = lax.rem(x + 2, SIDE)
        remote(h, kv, xx, yy, relay_send.at[h, kv, yy], relay_recv.at[h, kv, yy], right).wait_recv()

    def queries(h, i):
        c = h * 2 * HD
        return jnp.concatenate(
            [query[source[i], :, c:c + HD], query[source[i], :, c + HD:c + 2 * HD]], axis=0)

    def exponent(s):
        return jnp.exp(SOFTCAP * jnp.tanh(s * (HD ** -0.5 / SOFTCAP)))

    def first(h):
        c = h * HD
        row = lax.broadcasted_iota(jnp.int32, (2 * tokens, tokens), 0)
        key = lax.broadcasted_iota(jnp.int32, (2 * tokens, tokens), 1)
        allowed = key <= lax.rem(row, tokens)
        for i in range(3):
            kc = keyval[source[i], 0, :, c:c + HD]
            vc = keyval[source[i], 1, :, c:c + HD]
            s = lax.dot_general(queries(h, i), kc, NT, preferred_element_type=jnp.float32)
            e = jnp.where(allowed, exponent(s), 0.0)
            den[i] = e
            num[i] = jnp.dot(e.astype(jnp.bfloat16), vc, preferred_element_type=jnp.float32)

    def chunk(h, xx):
        part = pl.ds(pl.multiple_of(xx * col, col), col)
        for i in range(3):
            s = lax.dot_general(queries(h, i), kbuf[h, part], NT, preferred_element_type=jnp.float32)
            e = exponent(s)
            den[i] += e[:, :tokens] + e[:, tokens:]
            num[i] += jnp.dot(e.astype(jnp.bfloat16), vbuf[h, part], preferred_element_type=jnp.float32)

    def finish(h):
        for i in range(3):
            total = jnp.sum(den[i], axis=-1, keepdims=True)
            att = (num[i] / total).astype(jnp.bfloat16)
            for r in range(2):
                head = att[r * tokens:(r + 1) * tokens]
                c = (2 * h + r) * HD
                term = head[tokens - 1:].astype(jnp.float32) * weight_ref[:, c:c + HD].astype(jnp.float32)
                if h == 0 and r == 0:
                    sums[i] = term
                else:
                    sums[i] += term
                if i == 0:
                    sent[h, :, r * HD:(r + 1) * HD] = head * moved.astype(jnp.bfloat16)
                else:
                    own[i - 1, :, c:c + HD] = head
            if i == 0:
                guest_copy(h).start()

    def guest_copy(h):
        return pltpu.make_async_remote_copy(
            src_ref=sent.at[h], dst_ref=guest.at[h], send_sem=g_send.at[h], recv_sem=g_recv.at[h],
            device_id=ahead, device_id_type=MESH)

    pl.semaphore_wait(barrier, 7)

    def begin(h):
        for kv in range(2):
            loads[h * 2 + kv].wait()
            for d in (1, 3, 2):
                y_copy(h, kv, d).start()
            for side in range(2):
                x_copy(h, kv, y, side).start()

    def spread(h):
        for d in (1, 3, 2):
            for kv in range(2):
                yy = wait_y(h, kv, d)
                for side in range(2):
                    x_copy(h, kv, yy, side).start()

    def order(d):
        return lax.rem(y + d, SIDE)

    def pass_on(h, d):
        yy = order(d)
        wait_x(h, 0, yy, 0)
        relay_copy(h, 0, yy).start()
        wait_x(h, 1, yy, 1)
        relay_copy(h, 1, yy).start()

    for h in range(KVH):
        begin(h)
    loads[8].wait()
    loads[9].wait()
    spread(0)
    for h in range(KVH):
        first(h)
        if h + 1 < KVH:
            spread(h + 1)
        chunk(h, x)
        for d in (0, 1, 3, 2):
            pass_on(h, d)
        for d in (0, 1, 3, 2):
            wait_x(h, 1, order(d), 0)
        chunk(h, lax.rem(x + 3, SIDE))
        for d in (0, 1, 3, 2):
            wait_x(h, 0, order(d), 1)
        chunk(h, lax.rem(x + 1, SIDE))
        for d in (0, 1, 3, 2):
            for kv in range(2):
                wait_relay(h, kv, order(d))
        chunk(h, lax.rem(x + 2, SIDE))
        finish(h)

    slot = lax.broadcasted_iota(jnp.int32, (1, 3), 1)
    totals = [jnp.sum(sums[i], axis=-1, keepdims=True) for i in range(3)]
    place = slot - (slot > move).astype(jnp.int32)
    kept_score = jnp.where(place <= 0, totals[1], totals[2])
    score_ref[...] = jnp.where(
        slot == move, totals[0], jnp.where(slot < count, kept_score, 0.0))

    for h in range(KVH):
        guest_copy(h).wait_recv()
        for j in range(2):
            is_own = (kept > j).astype(jnp.bfloat16)
            is_guest = (kept == j).astype(jnp.bfloat16)
            c = h * 2 * HD
            att_ref[j, :, c:c + 2 * HD] = own[j, :, c:c + 2 * HD] * is_own + guest[h] * is_guest

    for h in range(KVH):
        guest_copy(h).wait_send()
        for kv in range(2):
            for d in (1, 2, 3):
                y_copy(h, kv, d).wait_send()
            for yy in range(SIDE):
                for side in range(2):
                    x_copy(h, kv, yy, side).wait_send()
                relay_copy(h, kv, yy).wait_send()


def body(
    passage_query, passage_keyval, prefix_keys, prefix_values, home_count, move_slot, score_weight
):
    query = passage_query[0, 0]
    keyval = passage_keyval[0, 0]
    slots, tokens, width = query.shape
    rows = prefix_keys.shape[1]
    lanes = lax.axis_size("lane")
    any_ = pl.BlockSpec(memory_space=pl.ANY)
    smem = pl.BlockSpec(memory_space=pltpu.SMEM)
    vmem = pl.BlockSpec(memory_space=pltpu.VMEM)
    bf16, f32 = jnp.bfloat16, jnp.float32
    dma = pltpu.SemaphoreType.DMA
    attended, scores = pl.pallas_call(
        kernel,
        out_shape=(
            jax.ShapeDtypeStruct((2, tokens, width), bf16),
            jax.ShapeDtypeStruct((1, slots), f32),
        ),
        in_specs=[any_, any_, any_, any_, smem, smem, vmem],
        out_specs=(vmem, vmem),
        scratch_shapes=[
            pltpu.VMEM((KVH, rows * lanes, HD), bf16),
            pltpu.VMEM((KVH, rows * lanes, HD), bf16),
            pltpu.VMEM(query.shape, bf16),
            pltpu.VMEM(keyval.shape, bf16),
            pltpu.VMEM((3, 2 * tokens, HD), f32),
            pltpu.VMEM((3, 2 * tokens, tokens), f32),
            pltpu.VMEM((2, tokens, width), bf16),
            pltpu.VMEM((KVH, tokens, 2 * HD), bf16),
            pltpu.VMEM((KVH, tokens, 2 * HD), bf16),
            pltpu.VMEM((3, 1, HD), f32),
            dma((10,)),
            dma((KVH, 2, 3)),
            dma((KVH, 2, SIDE, 2)),
            dma((KVH, 2, SIDE)),
            dma((KVH, 2, SIDE)),
            dma((KVH, 2, SIDE, 2)),
            dma((KVH, 2, SIDE)),
            dma((KVH,)),
            dma((KVH,)),
        ],
        compiler_params=pltpu.CompilerParams(
            collective_id=0, has_side_effects=True, vmem_limit_bytes=48 * 2**20),
    )(query, keyval, prefix_keys[0], prefix_values[0], home_count, move_slot, score_weight[None])
    return attended[None, None], scores[None]


def solution(mesh):
    in_specs = (
        P("grp", "lane", None, None, None),
        P("grp", "lane", None, None, None, None),
        P("grp", "lane", None),
        P("grp", "lane", None),
        P("grp", "lane"),
        P("grp", "lane"),
        P(),
    )
    out_specs = (P("grp", "lane", None, None, None), P("grp", "lane", None))
    return jax.shard_map(body, mesh=mesh, in_specs=in_specs, out_specs=out_specs, check_vma=False)
```

time: 420 us -> 75.4 us (0.18)
  the two profiles are of different devices: /device:TPU:1 before, /device:TPU:8 now
where the time goes in v1:
time: 75.4 us; the launch traced here: 75.1 us
  Pallas kernels  66.4 us (88%)
  local copies, waits for them, and re-layouts  6.8 us (9%)
  between operations  1.94 us (3%)
    pallas_call x1, Pallas kernels, body(): pl.pallas_call(kernel, out_shape=(jax.ShapeDtypeStruct((2, tokens, width)...  66.4 us
    unnamed x10, local copies, waits for them, and re-layouts  6.1 us

profile of v1, /device:TPU:8, one launch (start us, length us, event | category | flops | bytes accessed | tf_op | source)
XLA Modules:
  0.0 75.1 jit_solution(11833826260935891700)
XLA Ops:
  1.9 0.7 broadcast_in_dim.9.weight_ref
  2.6 0.0 copy-start
  2.6 1.4 %copy-done = bf16[1,1,3,128,2048]{4,3,2,1,0:T(8,128)(2,1)S(1)} copy-done((bf16[1,1,3,128,2048]{4,3,2,1,0:T(8,128)(2,1)S(1)}, bf16[1,1,3,128,2048]{4,3,2,1,0:T(8,128)(2,1)}, u32[]{:S(2)}) %copy-start) | copy-done | bytes 1572888
  4.0 0.0 copy-start.1
  4.0 1.4 %copy-done.1 = bf16[1,1,3,2,128,1024]{5,4,3,2,1,0:T(8,128)(2,1)S(1)} copy-done((bf16[1,1,3,2,128,1024]{5,4,3,2,1,0:T(8,128)(2,1)S(1)}, bf16[1,1,3,2,128,1024]{5,4,3,2,1,0:T(8,128)(2,1)}, u32[]{:S(2)}) %copy-start.1) | copy-done | bytes 1572888
  5.4 0.0 copy-start.2
  5.4 0.9 %copy-done.2 = bf16[1,64,1024]{2,1,0:T(8,128)(2,1)S(1)} copy-done((bf16[1,64,1024]{2,1,0:T(8,128)(2,1)S(1)}, bf16[1,64,1024]{2,1,0:T(8,128)(2,1)}, u32[]{:S(2)}) %copy-start.2) | copy-done | bytes 131096
  6.3 0.0 copy-start.3
  6.3 0.9 %copy-done.3 = bf16[1,64,1024]{2,1,0:T(8,128)(2,1)S(1)} copy-done((bf16[1,64,1024]{2,1,0:T(8,128)(2,1)S(1)}, bf16[1,64,1024]{2,1,0:T(8,128)(2,1)}, u32[]{:S(2)}) %copy-start.3) | copy-done | bytes 131096
  7.2 66.4 %shard_map.86 = (bf16[2,128,2048]{2,1,0:T(8,128)(2,1)S(1)}, f32[1,3]{1,0:T(1,128)S(1)}) custom-call(bf16[3,128,2048]{2,1,0:T(8,128)(2,1)S(1)} %bitcast.6, bf16[3,2,128,1024]{3,2,1,0:T(8,128)(2,1)S(1)} %bitcast.7, bf16[64,1024]{1,0:T(8,128)(2,1)S(1)} %bitcast.9, bf16[64,1024]{1,0:T(8,128)(2,1)S(1)} %bitcast.10, s32[1,1]{1,0:T(1,128)S(6)} %copy.11.count_ref, ...), custom_call_target="tpu_custom_call" | custom-call | tf_op jit(solution)/shard_map/pallas_call | solution.py:235
  73.6 1.0 %copy.13 = bf16[1,1,2,128,2048]{4,3,2,1,0:T(8,128)(2,1)} copy(bf16[1,1,2,128,2048]{4,3,2,1,0:T(8,128)(2,1)S(1)} %bitcast.8) | data formatting | bytes 2097152
  74.6 0.5 copy.14
Async XLA Ops:
  2.6 1.4 %copy-start = (bf16[1,1,3,128,2048]{4,3,2,1,0:T(8,128)(2,1)S(1)}, bf16[1,1,3,128,2048]{4,3,2,1,0:T(8,128)(2,1)}, u32[]{:S(2)}) copy-start(bf16[1,1,3,128,2048]{4,3,2,1,0:T(8,128)(2,1)} %param.7) | copy-start | bytes 4718596
  4.0 1.4 %copy-start.1 = (bf16[1,1,3,2,128,1024]{5,4,3,2,1,0:T(8,128)(2,1)S(1)}, bf16[1,1,3,2,128,1024]{5,4,3,2,1,0:T(8,128)(2,1)}, u32[]{:S(2)}) copy-start(bf16[1,1,3,2,128,1024]{5,4,3,2,1,0:T(8,128)(2,1)} %param.8) | copy-start | bytes 4718596
  5.4 0.9 %copy-start.2 = (bf16[1,64,1024]{2,1,0:T(8,128)(2,1)S(1)}, bf16[1,64,1024]{2,1,0:T(8,128)(2,1)}, u32[]{:S(2)}) copy-start(bf16[1,64,1024]{2,1,0:T(8,128)(2,1)} %param.9) | copy-start | bytes 393220
  6.3 0.9 %copy-start.3 = (bf16[1,64,1024]{2,1,0:T(8,128)(2,1)S(1)}, bf16[1,64,1024]{2,1,0:T(8,128)(2,1)}, u32[]{:S(2)}) copy-start(bf16[1,64,1024]{2,1,0:T(8,128)(2,1)} %param.10) | copy-start | bytes 393220

commit v2 on v1

--- a/solution.py
+++ b/solution.py
@@ -12,14 +12,16 @@
 KVH = 4
 SIDE = 4
 SOFTCAP = 50.0
+GY = 2
+GX = 5
 NT = (((1,), (1,)), ((), ()))
 
 
 def kernel(
     query_ref, keyval_ref, pkeys_ref, pvalues_ref, count_ref, move_ref, weight_ref,
     att_ref, score_ref,
-    kbuf, vbuf, query, keyval, num, den, own, sent, guest, sums,
-    load_sem, y_send, x_send, relay_send, y_recv, x_recv, relay_recv, g_send, g_recv,
+    kbuf, vbuf, query, keyval, num, den, own, sent, guest, transit, sums,
+    load_sem, y_send, x_send, relay_send, y_recv, x_recv, relay_recv, g_send, g_recv, t_send, t_recv, ready, hello, go, go_y,
 ):
     groups = lax.axis_size("grp")
     g = lax.axis_index("grp")
@@ -32,13 +34,32 @@
 
     right = (g, lax.rem(x + 1, SIDE) * SIDE + y)
     left = (g, lax.rem(x + 3, SIDE) * SIDE + y)
-    above = [(g, x * SIDE + lax.rem(y + d, SIDE)) for d in (1, 2, 3)]
+    across = [(g, x * SIDE + lax.rem(y + d, SIDE)) for d in (1, 2, 3)]
     ahead = (lax.rem(g + 1, groups), lane)
     behind = (lax.rem(g + groups - 1, groups), lane)
+    run = min(groups, 16)
+    odd = lax.rem(g, 2)
+    not_first = (lax.rem(g, run) > 0).astype(jnp.int32)
+    not_last = (lax.rem(g, run) < run - 1).astype(jnp.int32)
+    via = run > 2
+    is_via = lax.rem(g, run) == 1
+    closer = (g // run * run + run - 1, lane)
+    stop = (g // run * run + 1, lane)
+    landing = (lax.rem(g + run - 1, groups), lane)
+    near = (y + 1 - 2 * lax.rem(y, 2), 2 - y // 2, 3 - 3 * (y // 2))
 
     barrier = pltpu.get_barrier_semaphore()
-    for other in (right, left, *above, ahead, behind):
+
+    def greet(other):
         pl.semaphore_signal(barrier, inc=1, device_id=other, device_id_type=MESH)
+
+    for other in (right, left, *across):
+        greet(other)
+    pl.when(odd == 1)(lambda: greet(behind))
+    pl.when((odd == 1) & (not_last == 1))(lambda: greet(ahead))
+    pl.when((odd == 0) & (not_first == 0))(lambda: greet(behind))
+    if via:
+        pl.when(is_via)(lambda: greet(closer))
 
     def block(xx, yy):
         return pl.ds(pl.multiple_of((xx * SIDE + yy) * rows, rows), rows)
@@ -66,7 +87,7 @@
             device_id=to, device_id_type=MESH)
 
     def y_copy(h, kv, d):
-        return remote(h, kv, x, y, y_send.at[h, kv, d - 1], y_recv.at[h, kv, y], above[d - 1])
+        return remote(h, kv, x, y, y_send.at[h, kv, d], y_recv.at[h, kv, y], across[d])
 
     def x_copy(h, kv, yy, side):
         return remote(h, kv, x, yy, x_send.at[h, kv, yy, side], x_recv.at[h, kv, yy, side],
@@ -76,10 +97,8 @@
         xx = lax.rem(x + (3, 1)[kv], SIDE)
         return remote(h, kv, xx, yy, relay_send.at[h, kv, yy], relay_recv.at[h, kv, yy], (right, left)[kv])
 
-    def wait_y(h, kv, d):
-        yy = lax.rem(y + d, SIDE)
+    def wait_y(h, kv, yy):
         remote(h, kv, x, yy, y_send.at[h, kv, 0], y_recv.at[h, kv, yy], right).wait_recv()
-        return yy
 
     def wait_x(h, kv, yy, side):
         xx = lax.rem(x + (3, 1)[side], SIDE)
@@ -125,7 +144,7 @@
             for r in range(2):
                 head = att[r * tokens:(r + 1) * tokens]
                 c = (2 * h + r) * HD
-                term = head[tokens - 1:].astype(jnp.float32) * weight_ref[:, c:c + HD].astype(jnp.float32)
+                term = head[tokens - 1:].astype(jnp.float32) * weight_ref[pl.ds(c, HD)].astype(jnp.float32).reshape(1, HD)
                 if h == 0 and r == 0:
                     sums[i] = term
                 else:
@@ -135,63 +154,123 @@
                 else:
                     own[i - 1, :, c:c + HD] = head
             if i == 0:
-                guest_copy(h).start()
+                if via and h < KVH - 1:
+                    pl.when(not_last == 1)(lambda: guest_copy(h).start())
+                    pl.when(not_last == 0)(lambda: transit_copy(h).start())
+                else:
+                    guest_copy(h).start()
+
+    def transit_copy(h):
+        return pltpu.make_async_remote_copy(
+            src_ref=sent.at[h], dst_ref=transit.at[h], send_sem=g_send.at[h], recv_sem=t_recv.at[h],
+            device_id=stop, device_id_type=MESH)
+
+    def landing_copy(h):
+        return pltpu.make_async_remote_copy(
+            src_ref=transit.at[h], dst_ref=guest.at[h], send_sem=t_send.at[h], recv_sem=g_recv.at[h],
+            device_id=landing, device_id_type=MESH)
 
     def guest_copy(h):
         return pltpu.make_async_remote_copy(
             src_ref=sent.at[h], dst_ref=guest.at[h], send_sem=g_send.at[h], recv_sem=g_recv.at[h],
             device_id=ahead, device_id_type=MESH)
 
-    pl.semaphore_wait(barrier, 7)
+    pl.semaphore_wait(barrier, 5 + (1 - odd) * (1 + not_first) + odd * (1 - not_last) * (2 if via else 1))
+
+    def tell(sem, other):
+        pl.semaphore_signal(sem, inc=1, device_id=other, device_id_type=MESH)
+
+    @pl.when(odd == 0)
+    def _():
+        tell(hello, ahead)
+        pl.when(not_first == 1)(lambda: tell(ready, behind))
+
+    def release(sem):
+        pl.when(odd == 1)(lambda: tell(sem, behind))
 
     def begin(h):
         for kv in range(2):
             loads[h * 2 + kv].wait()
-            for d in (1, 3, 2):
+            for d in range(3):
                 y_copy(h, kv, d).start()
+
+    def begin_x(h):
+        for kv in range(2):
             for side in range(2):
                 x_copy(h, kv, y, side).start()
 
     def spread(h):
-        for d in (1, 3, 2):
+        for yy in near:
             for kv in range(2):
-                yy = wait_y(h, kv, d)
+                wait_y(h, kv, yy)
                 for side in range(2):
                     x_copy(h, kv, yy, side).start()
 
-    def order(d):
-        return lax.rem(y + d, SIDE)
-
-    def pass_on(h, d):
-        yy = order(d)
+    order = (y, *near)
+
+    def pass_on(h, i):
+        yy = order[i]
         wait_x(h, 0, yy, 0)
         relay_copy(h, 0, yy).start()
         wait_x(h, 1, yy, 1)
         relay_copy(h, 1, yy).start()
 
+    def work(h, i):
+        if i == 0:
+            first(h)
+            chunk(h, x)
+        if i == 1:
+            for yy in order:
+                wait_x(h, 1, yy, 0)
+            chunk(h, lax.rem(x + 3, SIDE))
+        if i == 2:
+            for yy in order:
+                wait_x(h, 0, yy, 1)
+            chunk(h, lax.rem(x + 1, SIDE))
+        if i == 3:
+            for yy in order:
+                for kv in range(2):
+                    wait_relay(h, kv, yy)
+            chunk(h, lax.rem(x + 2, SIDE))
+            if h == 0:
+                pl.when((odd == 1) & (not_last == 1))(lambda: pl.semaphore_wait(ready, 1))
+            finish(h)
+
+    pl.when((odd == 0) & (GY >= 0))(lambda: pl.semaphore_wait(go_y, 1))
     for h in range(KVH):
         begin(h)
+    pl.when(odd == 1)(lambda: pl.semaphore_wait(hello, 1))
+    pl.when((odd == 0) & (GX >= 0))(lambda: pl.semaphore_wait(go, 1))
+    for h in range(KVH):
+        begin_x(h)
+    for h in range(2):
+        spread(h)
+        if GY == h:
+            release(go_y)
+        if GX == h:
+            release(go)
     loads[8].wait()
     loads[9].wait()
-    spread(0)
-    for h in range(KVH):
-        first(h)
-        if h + 1 < KVH:
-            spread(h + 1)
-        chunk(h, x)
-        for d in (0, 1, 3, 2):
-            pass_on(h, d)
-        for d in (0, 1, 3, 2):
-            wait_x(h, 1, order(d), 0)
-        chunk(h, lax.rem(x + 3, SIDE))
-        for d in (0, 1, 3, 2):
-            wait_x(h, 0, order(d), 1)
-        chunk(h, lax.rem(x + 1, SIDE))
-        for d in (0, 1, 3, 2):
-            for kv in range(2):
-                wait_relay(h, kv, order(d))
-        chunk(h, lax.rem(x + 2, SIDE))
-        finish(h)
+    for h in range(KVH):
+        for i in range(SIDE):
+            pass_on(h, i)
+            if h > 0:
+                work(h - 1, i)
+        if GX == h + 4:
+            release(go)
+        if h + 2 < KVH:
+            spread(h + 2)
+            if GY == h + 2:
+                release(go_y)
+    for i in range(SIDE):
+        work(KVH - 1, i)
+
+    if via:
+        @pl.when(is_via)
+        def _():
+            for h in range(KVH - 1):
+                transit_copy(h).wait_recv()
+                landing_copy(h).start()
 
     slot = lax.broadcasted_iota(jnp.int32, (1, 3), 1)
     totals = [jnp.sum(sums[i], axis=-1, keepdims=True) for i in range(3)]
@@ -208,10 +287,16 @@
             c = h * 2 * HD
             att_ref[j, :, c:c + 2 * HD] = own[j, :, c:c + 2 * HD] * is_own + guest[h] * is_guest
 
+    if via:
+        @pl.when(is_via)
+        def _():
+            for h in range(KVH - 1):
+                landing_copy(h).wait_send()
+
     for h in range(KVH):
         guest_copy(h).wait_send()
         for kv in range(2):
-            for d in (1, 2, 3):
+            for d in range(3):
                 y_copy(h, kv, d).wait_send()
             for yy in range(SIDE):
                 for side in range(2):
@@ -228,7 +313,6 @@
     rows = prefix_keys.shape[1]
     lanes = lax.axis_size("lane")
     any_ = pl.BlockSpec(memory_space=pl.ANY)
-    smem = pl.BlockSpec(memory_space=pltpu.SMEM)
     vmem = pl.BlockSpec(memory_space=pltpu.VMEM)
     bf16, f32 = jnp.bfloat16, jnp.float32
     dma = pltpu.SemaphoreType.DMA
@@ -238,7 +322,7 @@
             jax.ShapeDtypeStruct((2, tokens, width), bf16),
             jax.ShapeDtypeStruct((1, slots), f32),
         ),
-        in_specs=[any_, any_, any_, any_, smem, smem, vmem],
+        in_specs=[any_, any_, any_, any_, vmem, vmem, vmem],
         out_specs=(vmem, vmem),
         scratch_shapes=[
             pltpu.VMEM((KVH, rows * lanes, HD), bf16),
@@ -250,6 +334,7 @@
             pltpu.VMEM((2, tokens, width), bf16),
             pltpu.VMEM((KVH, tokens, 2 * HD), bf16),
             pltpu.VMEM((KVH, tokens, 2 * HD), bf16),
+            pltpu.VMEM((KVH - 1, tokens, 2 * HD), bf16),
             pltpu.VMEM((3, 1, HD), f32),
             dma((10,)),
             dma((KVH, 2, 3)),
@@ -260,10 +345,16 @@
             dma((KVH, 2, SIDE)),
             dma((KVH,)),
             dma((KVH,)),
+            dma((KVH - 1,)),
+            dma((KVH - 1,)),
+            pltpu.SemaphoreType.REGULAR,
+            pltpu.SemaphoreType.REGULAR,
+            pltpu.SemaphoreType.REGULAR,
+            pltpu.SemaphoreType.REGULAR,
         ],
         compiler_params=pltpu.CompilerParams(
-            collective_id=0, has_side_effects=True, vmem_limit_bytes=48 * 2**20),
-    )(query, keyval, prefix_keys[0], prefix_values[0], home_count, move_slot, score_weight[None])
+            collective_id=0, has_side_effects=True, vmem_limit_bytes=60 * 2**20),
+    )(query, keyval, prefix_keys[0], prefix_values[0], home_count, move_slot, score_weight)
     return attended[None, None], scores[None]
 
 

time: 75.4 us -> 57.8 us (0.77)
  the two profiles are of different devices: /device:TPU:8 before, /device:TPU:1 now
where the time goes in v2:
time: 57.8 us; the launch traced here: 57.6 us
  Pallas kernels  52.8 us (91%)
  local copies, waits for them, and re-layouts  2.82 us (5%)
  between operations  1.94 us (3%)
    pallas_call x1, Pallas kernels, body(): pl.pallas_call(kernel, out_shape=(jax.ShapeDtypeStruct((2, tokens, width)...  52.8 us
    unnamed x4, local copies, waits for them, and re-layouts  2.82 us

profile of v2, /device:TPU:1, one launch (start us, length us, event | category | flops | bytes accessed | tf_op | source)
XLA Modules:
  0.0 57.6 jit_solution(5565349163902034891)
XLA Ops:
  1.9 52.8 %shard_map.86 = (bf16[2,128,2048]{2,1,0:T(8,128)(2,1)}, f32[1,3]{1,0:T(1,128)}) custom-call(bf16[3,128,2048]{2,1,0:T(8,128)(2,1)} %bitcast.6, bf16[3,2,128,1024]{3,2,1,0:T(8,128)(2,1)} %bitcast.7, bf16[64,1024]{1,0:T(8,128)(2,1)} %bitcast.9, bf16[64,1024]{1,0:T(8,128)(2,1)} %bitcast.10, s32[1,1]{1,0:T(1,128)S(6)} %copy.11.count_ref, ...), custom_call_target="tpu_custom_call" | custom-call | tf_op jit(solution)/shard_map/pallas_call | solution.py:319
  54.7 0.0 copy-start
  54.7 2.3 %copy.13 = bf16[1,1,2,128,2048]{4,3,2,1,0:T(8,128)(2,1)} copy(bf16[1,1,2,128,2048]{4,3,2,1,0:T(8,128)(2,1)} %bitcast.8) | data formatting | bytes 2097152
  57.1 0.0 copy-done
  57.1 0.5 copy.14
Async XLA Ops:
  54.7 2.3 %copy-start = (f32[1,3]{1,0:T(1,128)S(1)}, f32[1,3]{1,0:T(1,128)}, u32[]{:S(2)}) copy-start(f32[1,3]{1,0:T(1,128)} %get-tuple-element.5) | copy-start | bytes 40

commit v3 on v2

--- a/solution.py
+++ b/solution.py
@@ -13,7 +13,8 @@
 SIDE = 4
 SOFTCAP = 50.0
 GY = 2
-GX = 5
+VIA = 2
+GX = 6
 NT = (((1,), (1,)), ((), ()))
 
 
@@ -129,16 +130,16 @@
             den[i] = e
             num[i] = jnp.dot(e.astype(jnp.bfloat16), vc, preferred_element_type=jnp.float32)
 
-    def chunk(h, xx):
+    def chunk(h, xx, slots=(0, 1, 2)):
         part = pl.ds(pl.multiple_of(xx * col, col), col)
-        for i in range(3):
+        for i in slots:
             s = lax.dot_general(queries(h, i), kbuf[h, part], NT, preferred_element_type=jnp.float32)
             e = exponent(s)
             den[i] += e[:, :tokens] + e[:, tokens:]
             num[i] += jnp.dot(e.astype(jnp.bfloat16), vbuf[h, part], preferred_element_type=jnp.float32)
 
-    def finish(h):
-        for i in range(3):
+    def finish(h, slots):
+        for i in slots:
             total = jnp.sum(den[i], axis=-1, keepdims=True)
             att = (num[i] / total).astype(jnp.bfloat16)
             for r in range(2):
@@ -154,7 +155,7 @@
                 else:
                     own[i - 1, :, c:c + HD] = head
             if i == 0:
-                if via and h < KVH - 1:
+                if via and h < VIA:
                     pl.when(not_last == 1)(lambda: guest_copy(h).start())
                     pl.when(not_last == 0)(lambda: transit_copy(h).start())
                 else:
@@ -231,15 +232,15 @@
             for yy in order:
                 for kv in range(2):
                     wait_relay(h, kv, yy)
-            chunk(h, lax.rem(x + 2, SIDE))
             if h == 0:
                 pl.when((odd == 1) & (not_last == 1))(lambda: pl.semaphore_wait(ready, 1))
-            finish(h)
+            for slots in ((0,), (1, 2)):
+                chunk(h, lax.rem(x + 2, SIDE), slots)
+                finish(h, slots)
 
     pl.when((odd == 0) & (GY >= 0))(lambda: pl.semaphore_wait(go_y, 1))
     for h in range(KVH):
         begin(h)
-    pl.when(odd == 1)(lambda: pl.semaphore_wait(hello, 1))
     pl.when((odd == 0) & (GX >= 0))(lambda: pl.semaphore_wait(go, 1))
     for h in range(KVH):
         begin_x(h)
@@ -261,6 +262,7 @@
         if h + 2 < KVH:
             spread(h + 2)
             if GY == h + 2:
+                pl.when(odd == 1)(lambda: pl.semaphore_wait(hello, 1))
                 release(go_y)
     for i in range(SIDE):
         work(KVH - 1, i)
@@ -268,7 +270,7 @@
     if via:
         @pl.when(is_via)
         def _():
-            for h in range(KVH - 1):
+            for h in range(VIA):
                 transit_copy(h).wait_recv()
                 landing_copy(h).start()
 
@@ -290,7 +292,7 @@
     if via:
         @pl.when(is_via)
         def _():
-            for h in range(KVH - 1):
+            for h in range(VIA):
                 landing_copy(h).wait_send()
 
     for h in range(KVH):
@@ -319,8 +321,8 @@
     attended, scores = pl.pallas_call(
         kernel,
         out_shape=(
-            jax.ShapeDtypeStruct((2, tokens, width), bf16),
-            jax.ShapeDtypeStruct((1, slots), f32),
+            pltpu.VMEM((2, tokens, width), bf16),
+            pltpu.VMEM((1, slots), f32),
         ),
         in_specs=[any_, any_, any_, any_, vmem, vmem, vmem],
         out_specs=(vmem, vmem),
@@ -334,7 +336,7 @@
             pltpu.VMEM((2, tokens, width), bf16),
             pltpu.VMEM((KVH, tokens, 2 * HD), bf16),
             pltpu.VMEM((KVH, tokens, 2 * HD), bf16),
-            pltpu.VMEM((KVH - 1, tokens, 2 * HD), bf16),
+            pltpu.VMEM((VIA, tokens, 2 * HD), bf16),
             pltpu.VMEM((3, 1, HD), f32),
             dma((10,)),
             dma((KVH, 2, 3)),
@@ -345,8 +347,8 @@
             dma((KVH, 2, SIDE)),
             dma((KVH,)),
             dma((KVH,)),
-            dma((KVH - 1,)),
-            dma((KVH - 1,)),
+            dma((VIA,)),
+            dma((VIA,)),
             pltpu.SemaphoreType.REGULAR,
             pltpu.SemaphoreType.REGULAR,
             pltpu.SemaphoreType.REGULAR,

time: 57.8 us -> 54.2 us (0.938)
  Pallas kernels: 52.8 us -> 50.6 us
  local copies, waits for them, and re-layouts: 2.82 us -> 1.48 us
    pallas_call x1, Pallas kernels: 52.8 us -> 50.6 us  [body(): pl.pallas_call(kernel, out_shape=(pltpu.VMEM((2, tokens, width), bf16), p...]
    unnamed x4 -> x2, local copies, waits for them, and re-layouts: 2.82 us -> 1.48 us
where the time goes in v3:
time: 54.2 us; the launch traced here: 54 us
  Pallas kernels  50.6 us (93%)
  between operations  1.93 us (4%)
  local copies, waits for them, and re-layouts  1.48 us (3%)
    pallas_call x1, Pallas kernels, body(): pl.pallas_call(kernel, out_shape=(pltpu.VMEM((2, tokens, width), bf16), p...  50.6 us
    unnamed x2, local copies, waits for them, and re-layouts  1.48 us

profile of v3, /device:TPU:1, one launch (start us, length us, event | category | flops | bytes accessed | tf_op | source)
XLA Modules:
  0.0 54.0 jit_solution(2682647595129960718)
XLA Ops:
  1.9 50.6 %shard_map.86 = (bf16[2,128,2048]{2,1,0:T(8,128)(2,1)S(1)}, f32[1,3]{1,0:T(1,128)S(1)}) custom-call(bf16[3,128,2048]{2,1,0:T(8,128)(2,1)} %bitcast.8, bf16[3,2,128,1024]{3,2,1,0:T(8,128)(2,1)} %bitcast.9, bf16[64,1024]{1,0:T(8,128)(2,1)} %bitcast.10, bf16[64,1024]{1,0:T(8,128)(2,1)} %bitcast.11, s32[1,1]{1,0:T(1,128)S(6)} %copy.13.count_ref, ...), custom_call_target="tpu_custom_call" | custom-call | tf_op jit(solution)/shard_map/pallas_call | solution.py:321
  52.6 1.0 %copy.11 = bf16[1,1,2,128,2048]{4,3,2,1,0:T(8,128)(2,1)} copy(bf16[1,1,2,128,2048]{4,3,2,1,0:T(8,128)(2,1)S(1)} %bitcast.6) | data formatting | bytes 2097152
  53.5 0.5 copy.12

commit v4 on v3

--- a/solution.py
+++ b/solution.py
@@ -19,9 +19,9 @@
 
 
 def kernel(
-    query_ref, keyval_ref, pkeys_ref, pvalues_ref, count_ref, move_ref, weight_ref,
+    query_ref, keyval_ref, pkeys_ref, pvalues_ref, count_ref, move_ref, weight_hbm,
     att_ref, score_ref,
-    kbuf, vbuf, query, keyval, num, den, own, sent, guest, transit, sums,
+    kbuf, vbuf, query, keyval, num, den, own, sent, guest, transit, sums, weight_ref,
     load_sem, y_send, x_send, relay_send, y_recv, x_recv, relay_recv, g_send, g_recv, t_send, t_recv, ready, hello, go, go_y,
 ):
     groups = lax.axis_size("grp")
@@ -35,7 +35,6 @@
 
     right = (g, lax.rem(x + 1, SIDE) * SIDE + y)
     left = (g, lax.rem(x + 3, SIDE) * SIDE + y)
-    across = [(g, x * SIDE + lax.rem(y + d, SIDE)) for d in (1, 2, 3)]
     ahead = (lax.rem(g + 1, groups), lane)
     behind = (lax.rem(g + groups - 1, groups), lane)
     run = min(groups, 16)
@@ -48,6 +47,7 @@
     stop = (g // run * run + 1, lane)
     landing = (lax.rem(g + run - 1, groups), lane)
     near = (y + 1 - 2 * lax.rem(y, 2), 2 - y // 2, 3 - 3 * (y // 2))
+    across = [(g, x * SIDE + yy) for yy in near]
 
     barrier = pltpu.get_barrier_semaphore()
 
@@ -72,6 +72,7 @@
                 ref.at[:, pl.ds(h * HD, HD)], bufs[kv].at[h, block(x, y)], load_sem.at[h * 2 + kv]))
     loads.append(pltpu.make_async_copy(query_ref, query, load_sem.at[8]))
     loads.append(pltpu.make_async_copy(keyval_ref, keyval, load_sem.at[9]))
+    loads.append(pltpu.make_async_copy(weight_hbm, weight_ref, load_sem.at[10]))
     for c in loads:
         c.start()
 
@@ -190,13 +191,13 @@
         pl.when(odd == 1)(lambda: tell(sem, behind))
 
     def begin(h):
+        for d in range(3):
+            for kv in range(2):
+                y_copy(h, kv, d).start()
+
+    def begin_x(h):
         for kv in range(2):
             loads[h * 2 + kv].wait()
-            for d in range(3):
-                y_copy(h, kv, d).start()
-
-    def begin_x(h):
-        for kv in range(2):
             for side in range(2):
                 x_copy(h, kv, y, side).start()
 
@@ -238,12 +239,16 @@
                 chunk(h, lax.rem(x + 2, SIDE), slots)
                 finish(h, slots)
 
-    pl.when((odd == 0) & (GY >= 0))(lambda: pl.semaphore_wait(go_y, 1))
-    for h in range(KVH):
-        begin(h)
-    pl.when((odd == 0) & (GX >= 0))(lambda: pl.semaphore_wait(go, 1))
     for h in range(KVH):
         begin_x(h)
+        pl.when(odd == 1)(functools.partial(begin, h))
+    @pl.when(odd == 0)
+    def _():
+        pl.semaphore_wait(go_y, 1)
+        for h in range(KVH):
+            begin(h)
+        pl.semaphore_wait(go, 1)
+
     for h in range(2):
         spread(h)
         if GY == h:
@@ -252,6 +257,7 @@
             release(go)
     loads[8].wait()
     loads[9].wait()
+    loads[10].wait()
     for h in range(KVH):
         for i in range(SIDE):
             pass_on(h, i)
@@ -315,6 +321,7 @@
     rows = prefix_keys.shape[1]
     lanes = lax.axis_size("lane")
     any_ = pl.BlockSpec(memory_space=pl.ANY)
+    smem = pl.BlockSpec(memory_space=pltpu.SMEM)
     vmem = pl.BlockSpec(memory_space=pltpu.VMEM)
     bf16, f32 = jnp.bfloat16, jnp.float32
     dma = pltpu.SemaphoreType.DMA
@@ -324,7 +331,7 @@
             pltpu.VMEM((2, tokens, width), bf16),
             pltpu.VMEM((1, slots), f32),
         ),
-        in_specs=[any_, any_, any_, any_, vmem, vmem, vmem],
+        in_specs=[any_, any_, any_, any_, smem, smem, any_],
         out_specs=(vmem, vmem),
         scratch_shapes=[
             pltpu.VMEM((KVH, rows * lanes, HD), bf16),
@@ -338,7 +345,8 @@
             pltpu.VMEM((KVH, tokens, 2 * HD), bf16),
             pltpu.VMEM((VIA, tokens, 2 * HD), bf16),
             pltpu.VMEM((3, 1, HD), f32),
-            dma((10,)),
+            pltpu.VMEM(score_weight.shape, bf16),
+            dma((11,)),
             dma((KVH, 2, 3)),
             dma((KVH, 2, SIDE, 2)),
             dma((KVH, 2, SIDE)),

time: 54.2 us -> 51.4 us (0.948)
  Pallas kernels: 50.6 us -> 47.8 us
    pallas_call x1, Pallas kernels: 50.6 us -> 47.8 us  [body(): pl.pallas_call(kernel, out_shape=(pltpu.VMEM((2, tokens, width), bf16), p...]
where the time goes in v4:
time: 51.4 us; the launch traced here: 51.2 us
  Pallas kernels  47.8 us (93%)
  between operations  1.93 us (4%)
  local copies, waits for them, and re-layouts  1.48 us (3%)
    pallas_call x1, Pallas kernels, body(): pl.pallas_call(kernel, out_shape=(pltpu.VMEM((2, tokens, width), bf16), p...  47.8 us
    unnamed x2, local copies, waits for them, and re-layouts  1.48 us

profile of v4, /device:TPU:1, one launch (start us, length us, event | category | flops | bytes accessed | tf_op | source)
XLA Modules:
  0.0 51.2 jit_solution(1354144029568141485)
XLA Ops:
  1.9 47.8 %shard_map.86 = (bf16[2,128,2048]{2,1,0:T(8,128)(2,1)S(1)}, f32[1,3]{1,0:T(1,128)S(1)}) custom-call(bf16[3,128,2048]{2,1,0:T(8,128)(2,1)} %bitcast.8, bf16[3,2,128,1024]{3,2,1,0:T(8,128)(2,1)} %bitcast.9, bf16[64,1024]{1,0:T(8,128)(2,1)} %bitcast.10, bf16[64,1024]{1,0:T(8,128)(2,1)} %bitcast.11, s32[1,1]{1,0:T(1,128)S(6)} %copy.13.count_ref, ...), custom_call_target="tpu_custom_call" | custom-call | tf_op jit(solution)/shard_map/pallas_call | solution.py:328
  49.7 1.0 %copy.11 = bf16[1,1,2,128,2048]{4,3,2,1,0:T(8,128)(2,1)} copy(bf16[1,1,2,128,2048]{4,3,2,1,0:T(8,128)(2,1)S(1)} %bitcast.6) | data formatting | bytes 2097152
  50.7 0.5 copy.12

commit v5 on v4

--- a/solution.py
+++ b/solution.py
@@ -261,7 +261,7 @@
     for h in range(KVH):
         for i in range(SIDE):
             pass_on(h, i)
-            if h > 0:
+            if 0 < h < KVH - 1 or h > 0 and i < 2:
                 work(h - 1, i)
         if GX == h + 4:
             release(go)
@@ -270,6 +270,8 @@
             if GY == h + 2:
                 pl.when(odd == 1)(lambda: pl.semaphore_wait(hello, 1))
                 release(go_y)
+    work(KVH - 2, 2)
+    work(KVH - 2, 3)
     for i in range(SIDE):
         work(KVH - 1, i)
 
@@ -288,21 +290,6 @@
         slot == move, totals[0], jnp.where(slot < count, kept_score, 0.0))
 
     for h in range(KVH):
-        guest_copy(h).wait_recv()
-        for j in range(2):
-            is_own = (kept > j).astype(jnp.bfloat16)
-            is_guest = (kept == j).astype(jnp.bfloat16)
-            c = h * 2 * HD
-            att_ref[j, :, c:c + 2 * HD] = own[j, :, c:c + 2 * HD] * is_own + guest[h] * is_guest
-
-    if via:
-        @pl.when(is_via)
-        def _():
-            for h in range(VIA):
-                landing_copy(h).wait_send()
-
-    for h in range(KVH):
-        guest_copy(h).wait_send()
         for kv in range(2):
             for d in range(3):
                 y_copy(h, kv, d).wait_send()
@@ -310,6 +297,23 @@
                 for side in range(2):
                     x_copy(h, kv, yy, side).wait_send()
                 relay_copy(h, kv, yy).wait_send()
+
+    for h in range(KVH):
+        guest_copy(h).wait_recv()
+        for j in range(2):
+            is_own = (kept > j).astype(jnp.bfloat16)
+            is_guest = (kept == j).astype(jnp.bfloat16)
+            c = h * 2 * HD
+            att_ref[j, :, c:c + 2 * HD] = own[j, :, c:c + 2 * HD] * is_own + guest[h] * is_guest
+
+    if via:
+        @pl.when(is_via)
+        def _():
+            for h in range(VIA):
+                landing_copy(h).wait_send()
+
+    for h in range(KVH):
+        guest_copy(h).wait_send()
 
 
 def body(

time: 51.4 us -> 51.2 us (level)
  no operation moved by 1% of the time
where the time goes in v5:
time: 51.2 us; the launch traced here: 51 us
  Pallas kernels  47.6 us (93%)
  between operations  1.93 us (4%)
  local copies, waits for them, and re-layouts  1.48 us (3%)
    pallas_call x1, Pallas kernels, body(): pl.pallas_call(kernel, out_shape=(pltpu.VMEM((2, tokens, width), bf16), p...  47.6 us
    unnamed x2, local copies, waits for them, and re-layouts  1.48 us

profile of v5, /device:TPU:1, one launch (start us, length us, event | category | flops | bytes accessed | tf_op | source)
XLA Modules:
  0.0 51.0 jit_solution(14262592835366667958)
XLA Ops:
  1.9 47.6 %shard_map.86 = (bf16[2,128,2048]{2,1,0:T(8,128)(2,1)S(1)}, f32[1,3]{1,0:T(1,128)S(1)}) custom-call(bf16[3,128,2048]{2,1,0:T(8,128)(2,1)} %bitcast.8, bf16[3,2,128,1024]{3,2,1,0:T(8,128)(2,1)} %bitcast.9, bf16[64,1024]{1,0:T(8,128)(2,1)} %bitcast.10, bf16[64,1024]{1,0:T(8,128)(2,1)} %bitcast.11, s32[1,1]{1,0:T(1,128)S(6)} %copy.13.count_ref, ...), custom_call_target="tpu_custom_call" | custom-call | tf_op jit(solution)/shard_map/pallas_call | solution.py:332
  49.5 1.0 %copy.11 = bf16[1,1,2,128,2048]{4,3,2,1,0:T(8,128)(2,1)} copy(bf16[1,1,2,128,2048]{4,3,2,1,0:T(8,128)(2,1)S(1)} %bitcast.6) | data formatting | bytes 2097152
  50.5 0.5 copy.12
